TPU v7x, 256 devices: a whole 4x4x8 slice. The times are simulated.
256 devices in a mesh: img: 128 (over y, x, z), chan: 2 (over core).
Axes of the slice: x: 4, y: 4, z: 8, core: 2. Of those that a mesh axis runs over, the one named last changes fastest.
Arguments:
- visibilities: bfloat16 [2, 2, 2097152], P('chan', None, 'img'), may hold values from -6 to 6
- owner: int32 [2, 2097152, 1], P('chan', 'img'), may hold values from 0 to 127; in each aligned block of 16384 rows (0 to 16383, 16384 to 32767, ..., all dimensions but the last counted through in order) at most 256 rows name the same one
- cells: int32 [2, 2, 2097152], P('chan', None, 'img'), may hold values from 0 to 248
- taps: int32 [2, 2, 2097152], P('chan', None, 'img'), may hold values from 0 to 127
- kernel: bfloat16 [128, 8], replicated, may hold values from 0.099609375 to 1
- taper_rows: float32 [32768], P('img'), may hold values from 0.1 to 1.9
- taper_cols: float32 [256], P('chan'), may hold values from 0.1 to 1.9
Outputs:
- image: float32 [2, 32768, 256], P(None, 'img', 'chan')
Inputs may be any that keep to these rules, and one draw needn't show every extreme that they name: `owner`: among the visibilities of one channel held by one device, no subgrid is named more than 256 times, and in some device's rows one subgrid is named exactly 256 times.
All inputs are finite; a program needn't handle non-finite values.
Results may differ from a plain program's by a relative error of at most 0.0029.
Values may be sent and summed in bfloat16 or wider, within the bound.
A program may use at most 128 MiB of HBM per device.

v0:
```python
import math

import jax
import jax.numpy as jnp
from jax import lax
from jax.sharding import PartitionSpec as P

SUB = 256
TAPS = 8
OS = 128


def from_partner(value, axis, apart):
    mask = 2**apart
    pairs = [(source, source ^ mask) for source in range(lax.axis_size(axis))]
    return lax.ppermute(value, axis, pairs)


def dft_tables(length):
    positions = jnp.arange(length, dtype=jnp.int32)
    product = positions[:, None] * positions[None, :] % length
    angle_grid = product.astype(jnp.float32) * (2.0 * math.pi / length)
    return (jnp.cos(angle_grid), jnp.sin(angle_grid))


def exact_dot(left_side, right_side):
    return jnp.dot(
        left_side, right_side, precision=lax.Precision.HIGHEST, preferred_element_type=jnp.float32
    )


def transform_left(cosine, sine, real_part, imag_part):
    new_real = exact_dot(cosine, real_part) - exact_dot(sine, imag_part)
    new_imag = exact_dot(sine, real_part) + exact_dot(cosine, imag_part)
    return (new_real, new_imag)


def weighted_payload(vis_pair, tap_pair, kernel):
    one_hot_taps = (tap_pair[:, :, None] == jnp.arange(OS, dtype=jnp.int32)).astype(jnp.bfloat16)
    looked_up = jnp.einsum("prk,kt->ptr", one_hot_taps, kernel, preferred_element_type=jnp.float32)
    vis_float = vis_pair.astype(jnp.float32)
    weight_re = (vis_float[0][None, :] * looked_up[0]).astype(jnp.bfloat16)
    weight_im = (vis_float[1][None, :] * looked_up[0]).astype(jnp.bfloat16)
    return jnp.concatenate([weight_re, weight_im, looked_up[1].astype(jnp.bfloat16)], axis=0)


def dense_footprint(weights, starts, across):
    u_gap = across[None, :] - starts[:, None]
    dense = jnp.zeros(u_gap.shape, jnp.bfloat16)
    zero_value = jnp.zeros((), jnp.bfloat16)
    for tap_index in range(TAPS):
        dense = dense + jnp.where(u_gap == tap_index, weights[tap_index][:, None], zero_value)
    return dense


def radix_sections(spectrum, side):
    img_count = lax.axis_size("img")
    my_index = lax.axis_index("img")
    bit_count = img_count.bit_length() - 1
    local_rows = jnp.arange(side, dtype=jnp.int32)[:, None]
    for section_index in range(bit_count):
        bit_index = bit_count - 1 - section_index
        half_span = 1 << bit_index
        partner = from_partner(spectrum, "img", bit_index)
        upper_side = my_index >> bit_index & 1
        position = (my_index & half_span - 1) * side + local_rows
        angle_rot = position.astype(jnp.float32) * (2.0 * math.pi / (2 * half_span * side))
        cosine = jnp.cos(angle_rot)
        sine = jnp.sin(angle_rot)
        diff_re = partner[0] - spectrum[0]
        diff_im = partner[1] - spectrum[1]
        rotated = jnp.stack([diff_re * cosine - diff_im * sine, diff_re * sine + diff_im * cosine])
        spectrum = jnp.where(upper_side == 1, rotated, spectrum + partner)
    return spectrum


def body(visibilities, owner, cells, taps, kernel, taper_rows, taper_cols):
    img_count = lax.axis_size("img")
    vis_rows = visibilities.shape[2]
    capacity = 2 * vis_rows // img_count
    slot_count = img_count * capacity
    owners = owner[0, :, 0]
    one_hot_owner = (owners[:, None] == jnp.arange(img_count, dtype=jnp.int32)).astype(jnp.int32)
    slot_rank = jnp.cumsum(one_hot_owner, axis=0) - 1
    row_slot = jnp.sum(slot_rank * one_hot_owner, axis=1)
    target = owners * capacity + row_slot
    block_size = math.gcd(slot_count, 2048)
    across = jnp.arange(SUB, dtype=jnp.int32)
    outgoing = jnp.zeros((2, slot_count), jnp.bfloat16).at[:, target].set(visibilities[0])
    descriptors = jnp.concatenate([cells[0], taps[0]], axis=0)
    placing = jnp.zeros((4, slot_count), jnp.int32).at[:, target].set(descriptors)
    arrived, arrived_ints = (
        lax.all_to_all(
            outgoing.reshape(2, img_count, capacity), "img", split_axis=1, concat_axis=1, tiled=True
        ),
        lax.all_to_all(
            placing.reshape(4, img_count, capacity), "img", split_axis=1, concat_axis=1, tiled=True
        ),
    )
    arrived = arrived.reshape(2, slot_count)
    arrived_ints = arrived_ints.reshape(4, slot_count)

    def block_inputs(offset_row):
        block_vis = lax.dynamic_slice_in_dim(arrived, offset_row, block_size, 1)
        block_ints = lax.dynamic_slice_in_dim(arrived_ints, offset_row, block_size, 1)
        block_rows = weighted_payload(block_vis, block_ints[2:4], kernel)
        return (block_rows, block_ints[0:2])

    def accumulate(turn_index, subgrid):
        block_rows, block_cells = block_inputs(turn_index * block_size)
        dense_re = dense_footprint(block_rows[0:TAPS], block_cells[0], across)
        dense_im = dense_footprint(block_rows[TAPS : 2 * TAPS], block_cells[0], across)
        dense_v = dense_footprint(block_rows[2 * TAPS : 3 * TAPS], block_cells[1], across)
        u_dense = jnp.concatenate([dense_re, dense_im], axis=1)
        return subgrid + lax.dot_general(
            u_dense, dense_v, (((0,), (0,)), ((), ())), preferred_element_type=jnp.float32
        )

    subgrid = lax.fori_loop(
        0, slot_count // block_size, accumulate, jnp.zeros((2 * SUB, SUB), jnp.float32)
    )
    cosine, sine = dft_tables(SUB)
    grid_re = subgrid[:SUB]
    grid_im = subgrid[SUB:]
    spectrum = jnp.stack(
        [
            exact_dot(grid_re, cosine) - exact_dot(grid_im, sine),
            exact_dot(grid_re, sine) + exact_dot(grid_im, cosine),
        ]
    )
    spectrum = radix_sections(spectrum, SUB)
    final_re, final_im = transform_left(cosine, sine, spectrum[0], spectrum[1])
    spectrum = jnp.stack([final_re, final_im])
    spectrum = lax.psum_scatter(spectrum, "chan", scatter_dimension=2, tiled=True)
    scale = 1.0 / math.sqrt(SUB * img_count * SUB)
    return spectrum * taper_rows[None, :, None] * taper_cols[None, None, :] * scale


def solution(mesh):
    return jax.shard_map(
        body,
        mesh=mesh,
        in_specs=(
            P("chan", None, "img"),
            P("chan", "img", None),
            P("chan", None, "img"),
            P("chan", None, "img"),
            P(),
            P("img"),
            P("chan"),
        ),
        out_specs=P(None, "img", "chan"),
        check_vma=False,
    )
```

profile of v0, /device:TPU:1, one launch (start us, length us, event | category | flops | bytes accessed | tf_op | source)
XLA Modules:
  0.0 533.4 jit_solution(17425382270299352884)
XLA Ops:
  12.1 8.4 %add_add_fusion = s32[128,128,128]{1,0,2:T(8,128)} fusion(s32[128,128,128]{1,0,2:T(8,128)} %copy-done, s32[128,128]{1,0:T(8,128)S(1)} %copy.25), kind=kLoop, calls=%fused_computation.134 | loop fusion | flops 4194304 | bytes 16842752 | tf_op jit(solution)/shard_map/sub | solution.py:84
  20.5 9.3 %copy.26 = s32[128,128,128]{0,2,1:T(8,128)} copy(s32[128,128,128]{1,0,2:T(8,128)} %add_add_fusion) | data formatting | bytes 16777216 | tf_op jit(solution)/shard_map/sub | solution.py:84
  29.8 8.3 %fusion.108 = s32[16384]{0:T(1024)S(1)} fusion(s32[128,128,128]{0,2,1:T(8,128)} %copy.26, s32[16384]{0:T(1024)S(1)} %bitcast.103), kind=kLoop, calls=%fused_computation.133 | loop fusion | flops 6275072 | bytes 8519680 | tf_op jit(solution)/shard_map/reduce_sum | solution.py:85
  38.3 3.5 copy.29
  41.7 46.3 %scatter_custom_fusion.1 = bf16[2,32768]{0,1:T(8,128)(2,1)} fusion(s32[16384]{0:T(1024)S(1)} %bitcast.110, bf16[16384,2]{1,0:T(8,128)(2,1)} %copy.29, bf16[]{:T(256)} %constant.133.clone.1), kind=kCustom, calls=%fused_computation.141 | custom fusion | bytes 131584 | tf_op jit(solution)/shard_map/scatter | solution.py:89
  88.0 7.0 %copy.30 = bf16[2,128,256]{2,0,1:T(2,128)(2,1)} copy(bf16[2,128,256]{0,2,1:T(8,128)(2,1)} %bitcast.91) | data formatting | bytes 262144 | tf_op jit(solution)/shard_map/reshape | solution.py:94
  95.0 29.1 %all-to-all-start.1 = ((bf16[2,128,256]{2,0,1:T(2,128)(2,1)}), bf16[2,128,256]{2,0,1:T(2,128)(2,1)S(1)}, u32[]{:S(2)}, u32[]{:S(2)}) async-start(bf16[2,128,256]{2,0,1:T(2,128)(2,1)} %copy.30), calls=%async_computation.1 | async-start | bytes 262144 | tf_op jit(solution)/shard_map/all_to_all | solution.py:93
  124.3 5.1 copy.27
  129.4 47.4 %scatter_custom_fusion = s32[4,32768]{0,1:T(8,128)} fusion(s32[16384]{0:T(1024)S(1)} %bitcast.111, s32[16384,4]{1,0:T(8,128)} %copy.27, s32[]{:T(128)} %constant.120.clone.1), kind=kCustom, calls=%fused_computation.139 | custom fusion | bytes 524800 | tf_op jit(solution)/shard_map/scatter | solution.py:91
  176.8 9.9 %copy.28 = s32[4,128,256]{2,0,1:T(4,128)} copy(s32[4,128,256]{0,2,1:T(8,128)} %bitcast.90) | data formatting | bytes 1048576 | tf_op jit(solution)/shard_map/reshape | solution.py:97
  186.6 13.2 %all-to-all-start = ((s32[4,128,256]{2,0,1:T(4,128)}), s32[4,128,256]{2,0,1:T(4,128)S(1)}, u32[]{:S(2)}, u32[]{:S(2)}) async-start(s32[4,128,256]{2,0,1:T(4,128)} %copy.28), calls=%async_computation | async-start | bytes 1048576 | tf_op jit(solution)/shard_map/all_to_all | solution.py:96
  199.8 18.6 %all-to-all-done = s32[4,128,256]{2,0,1:T(4,128)S(1)} async-done(((s32[4,128,256]{2,0,1:T(4,128)}), s32[4,128,256]{2,0,1:T(4,128)S(1)}, u32[]{:S(2)}, u32[]{:S(2)}) %all-to-all-start) | async-done | bytes 524320 | tf_op jit(solution)/shard_map/all_to_all | solution.py:96
  218.5 173.4 %while.15 = (s32[]{:T(128)}, f32[512,256]{1,0:T(8,128)S(1)}, s32[4,32768]{1,0:T(4,128)S(1)}, bf16[2,32768]{1,0:T(2,128)(2,1)S(1)}, bf16[128,8]{0,1:T(8,128)(2,1)...) while((s32[]{:T(128)}, f32[512,256]{1,0:T(8,128)S(1)}, ...), condition=%wide.region_6.7_spmd.clone.clone, body=%wide.region_5.6_spmd.clone.clone.sunk | while | flops 597528576 | bytes 6039757 | solution.py:119
  220.4 5.3 fusion.205
  225.9 3.4 fusion.206
  231.2 5.3 fusion.205
  236.7 3.4 fusion.206
  242.1 5.3 fusion.205
  247.6 3.4 fusion.206
  252.9 5.3 fusion.205
  258.4 3.4 fusion.206
  263.7 5.3 fusion.205
  269.3 3.4 fusion.206
  274.6 5.3 fusion.205
  280.1 3.4 fusion.206
  285.4 5.3 fusion.205
  290.9 3.4 fusion.206
  296.3 5.3 fusion.205
  301.8 3.4 fusion.206
  307.1 5.3 fusion.205
  317.9 5.3 fusion.205
  328.8 5.3 fusion.205
  334.3 3.4 fusion.206
  339.6 5.3 fusion.205
  350.5 5.3 fusion.205
  361.3 5.3 fusion.205
  366.8 3.4 fusion.206
  372.1 5.3 fusion.205
  383.0 5.3 fusion.205
  397.6 11.8 %collective-permute-done = f32[2,256,256]{2,1,0:T(8,128)S(1)} collective-permute-done((f32[2,256,256]{2,1,0:T(8,128)S(1)}, f32[2,256,256]{2,1,0:T(8,128)S(1)}, u32[]{:S(2)}, u32[]{:S(2)}) %collective-permute-start) | collective-permute-done | bytes 524320 | tf_op jit(solution)/shard_map/ppermute | solution.py:16
  410.0 9.4 %collective-permute-done.1 = f32[2,256,256]{2,1,0:T(8,128)S(1)} collective-permute-done((f32[2,256,256]{2,1,0:T(8,128)S(1)}, f32[2,256,256]{2,1,0:T(8,128)S(1)}, u32[]{:S(2)}, u32[]{:S(2)}) %collective-permute-start.1) | collective-permute-done | bytes 524320 | tf_op jit(solution)/shard_map/ppermute | solution.py:16
  419.9 10.0 %collective-permute-done.2 = f32[2,256,256]{2,1,0:T(8,128)S(1)} collective-permute-done((f32[2,256,256]{2,1,0:T(8,128)S(1)}, f32[2,256,256]{2,1,0:T(8,128)S(1)}, u32[]{:S(2)}, u32[]{:S(2)}) %collective-permute-start.2) | collective-permute-done | bytes 524320 | tf_op jit(solution)/shard_map/ppermute | solution.py:16
  430.3 8.3 %collective-permute-done.3 = f32[2,256,256]{2,1,0:T(8,128)S(1)} collective-permute-done((f32[2,256,256]{2,1,0:T(8,128)S(1)}, f32[2,256,256]{2,1,0:T(8,128)S(1)}, u32[]{:S(2)}, u32[]{:S(2)}) %collective-permute-start.3) | collective-permute-done | bytes 524320 | tf_op jit(solution)/shard_map/ppermute | solution.py:16
  438.8 5.6 %collective-permute-start.4 = (f32[2,256,256]{2,1,0:T(8,128)S(1)}, f32[2,256,256]{2,1,0:T(8,128)S(1)}, u32[]{:S(2)}, u32[]{:S(2)}) collective-permute-start(f32[2,256,256]{2,1,0:T(8,128)S(1)} %maximum_select_fusion.3), channel_id=1, source_target_pairs={{0,8},{2,10},{4,12},{6,14},{8,0},{10,2},{12,4},{14,6},{16,24},{18,... | collective-permute-start | bytes 1572872 | tf_op jit(solution)/shard_map/ppermute | solution.py:16
  444.5 18.8 %collective-permute-done.4 = f32[2,256,256]{2,1,0:T(8,128)S(1)} collective-permute-done((f32[2,256,256]{2,1,0:T(8,128)S(1)}, f32[2,256,256]{2,1,0:T(8,128)S(1)}, u32[]{:S(2)}, u32[]{:S(2)}) %collective-permute-start.4) | collective-permute-done | bytes 524320 | tf_op jit(solution)/shard_map/ppermute | solution.py:16
  463.7 27.7 %collective-permute-done.5 = f32[2,256,256]{2,1,0:T(8,128)S(1)} collective-permute-done((f32[2,256,256]{2,1,0:T(8,128)S(1)}, f32[2,256,256]{2,1,0:T(8,128)S(1)}, u32[]{:S(2)}, u32[]{:S(2)}) %collective-permute-start.5) | collective-permute-done | bytes 524320 | tf_op jit(solution)/shard_map/ppermute | solution.py:16
  491.9 12.7 %collective-permute-done.6 = f32[2,256,256]{2,1,0:T(8,128)S(1)} collective-permute-done((f32[2,256,256]{2,1,0:T(8,128)S(1)}, f32[2,256,256]{2,1,0:T(8,128)S(1)}, u32[]{:S(2)}, u32[]{:S(2)}) %collective-permute-start.6) | collective-permute-done | bytes 524320 | tf_op jit(solution)/shard_map/ppermute | solution.py:16
  511.2 13.2 %reduce-scatter.2.cloned.1.call-done = f32[2,256,128]{2,1,0:T(8,128)} async-done(((f32[2,256,256]{2,1,0:T(8,128)}), f32[2,256,128]{2,1,0:T(8,128)}) %reduce-scatter.2.cloned.1.call-update) | async-done | bytes 262160 | tf_op jit(solution)/shard_map/reduce_scatter | solution.py:134
  (201 shorter events, 75.7 us)
Async XLA Ops:
  8.5 3.2 copy-start
  20.5 9.3 %copy-start.1 = (s32[1,16384,1]{1,2,0:T(1,128)S(1)}, s32[1,16384,1]{1,2,0:T(1,128)}, u32[]{:S(2)}) copy-start(s32[1,16384,1]{1,2,0:T(1,128)} %param.10) | copy-start | bytes 196612
  29.8 8.5 %copy-start.4 = (bf16[1,2,16384]{2,1,0:T(2,128)(2,1)S(1)}, bf16[1,2,16384]{2,1,0:T(2,128)(2,1)}, u32[]{:S(2)}) copy-start(bf16[1,2,16384]{2,1,0:T(2,128)(2,1)} %param.9) | copy-start | bytes 196612
  88.0 36.2 %copy-start.2 = (s32[1,2,16384]{2,1,0:T(2,128)S(1)}, s32[1,2,16384]{2,1,0:T(2,128)}, u32[]{:S(2)}) copy-start(s32[1,2,16384]{2,1,0:T(2,128)} %param.12) | copy-start | bytes 393220
  88.0 36.2 %copy-start.3 = (s32[1,2,16384]{2,1,0:T(2,128)S(1)}, s32[1,2,16384]{2,1,0:T(2,128)}, u32[]{:S(2)}) copy-start(s32[1,2,16384]{2,1,0:T(2,128)} %param.11) | copy-start | bytes 393220
  95.0 91.6 %all-to-all-start.1 = ((bf16[2,128,256]{2,0,1:T(2,128)(2,1)}), bf16[2,128,256]{2,0,1:T(2,128)(2,1)S(1)}, u32[]{:S(2)}, u32[]{:S(2)}) async-start(bf16[2,128,256]{2,0,1:T(2,128)(2,1)} %copy.30), calls=%async_computation.1 | async-start | bytes 262144 | tf_op jit(solution)/shard_map/all_to_all | solution.py:93
  176.7 41.7 %copy-start.7 = (bf16[128,8]{0,1:T(8,128)(2,1)S(1)}, bf16[128,8]{0,1:T(8,128)(2,1)}, u32[]{:S(2)}) copy-start(bf16[128,8]{0,1:T(8,128)(2,1)} %param.13) | copy-start | bytes 6148
  186.6 31.9 %all-to-all-start = ((s32[4,128,256]{2,0,1:T(4,128)}), s32[4,128,256]{2,0,1:T(4,128)S(1)}, u32[]{:S(2)}, u32[]{:S(2)}) async-start(s32[4,128,256]{2,0,1:T(4,128)} %copy.28), calls=%async_computation | async-start | bytes 1048576 | tf_op jit(solution)/shard_map/all_to_all | solution.py:96
  199.8 324.6 %reduce-scatter.2.cloned.1.call-start = ((), (), s32[]{:S(2)}) async-start(), calls=%async_computation.3 | async-start | bytes 786432 | tf_op jit(solution)/shard_map/reduce_scatter | solution.py:134
  397.4 12.1 %collective-permute-start = (f32[2,256,256]{2,1,0:T(8,128)S(1)}, f32[2,256,256]{2,1,0:T(8,128)S(1)}, u32[]{:S(2)}, u32[]{:S(2)}) collective-permute-start(f32[2,256,256]{2,1,0:T(8,128)S(1)} %pad_maximum_fusion), channel_id=1, source_target_pairs={{0,128},{2,130},{4,132},{6,134},{8,136},{10,138},{12,140},{14,142}... | collective-permute-start | bytes 1572872 | tf_op jit(solution)/shard_map/ppermute | solution.py:16
  409.7 9.7 %collective-permute-start.1 = (f32[2,256,256]{2,1,0:T(8,128)S(1)}, f32[2,256,256]{2,1,0:T(8,128)S(1)}, u32[]{:S(2)}, u32[]{:S(2)}) collective-permute-start(f32[2,256,256]{2,1,0:T(8,128)S(1)} %maximum_select_fusion), channel_id=1, source_target_pairs={{0,64},{2,66},{4,68},{6,70},{8,72},{10,74},{12,76},{14,78},{16,80}... | collective-permute-start | bytes 1572872 | tf_op jit(solution)/shard_map/ppermute | solution.py:16
  419.8 10.1 %collective-permute-start.2 = (f32[2,256,256]{2,1,0:T(8,128)S(1)}, f32[2,256,256]{2,1,0:T(8,128)S(1)}, u32[]{:S(2)}, u32[]{:S(2)}) collective-permute-start(f32[2,256,256]{2,1,0:T(8,128)S(1)} %maximum_select_fusion.1), channel_id=1, source_target_pairs={{0,32},{2,34},{4,36},{6,38},{8,40},{10,42},{12,44},{14,46},{16,48}... | collective-permute-start | bytes 1572872 | tf_op jit(solution)/shard_map/ppermute | solution.py:16
  430.2 8.4 %collective-permute-start.3 = (f32[2,256,256]{2,1,0:T(8,128)S(1)}, f32[2,256,256]{2,1,0:T(8,128)S(1)}, u32[]{:S(2)}, u32[]{:S(2)}) collective-permute-start(f32[2,256,256]{2,1,0:T(8,128)S(1)} %maximum_select_fusion.2), channel_id=1, source_target_pairs={{0,16},{2,18},{4,20},{6,22},{8,24},{10,26},{12,28},{14,30},{16,0},... | collective-permute-start | bytes 1572872 | tf_op jit(solution)/shard_map/ppermute | solution.py:16
  438.8 24.5 %collective-permute-start.4 = (f32[2,256,256]{2,1,0:T(8,128)S(1)}, f32[2,256,256]{2,1,0:T(8,128)S(1)}, u32[]{:S(2)}, u32[]{:S(2)}) collective-permute-start(f32[2,256,256]{2,1,0:T(8,128)S(1)} %maximum_select_fusion.3), channel_id=1, source_target_pairs={{0,8},{2,10},{4,12},{6,14},{8,0},{10,2},{12,4},{14,6},{16,24},{18,... | collective-permute-start | bytes 1572872 | tf_op jit(solution)/shard_map/ppermute | solution.py:16
  463.6 27.9 %collective-permute-start.5 = (f32[2,256,256]{2,1,0:T(8,128)S(1)}, f32[2,256,256]{2,1,0:T(8,128)S(1)}, u32[]{:S(2)}, u32[]{:S(2)}) collective-permute-start(f32[2,256,256]{2,1,0:T(8,128)S(1)} %maximum_select_fusion.4), channel_id=1, source_target_pairs={{0,4},{2,6},{4,0},{6,2},{8,12},{10,14},{12,8},{14,10},{16,20},{18,... | collective-permute-start | bytes 1572872 | tf_op jit(solution)/shard_map/ppermute | solution.py:16
  491.7 12.8 %collective-permute-start.6 = (f32[2,256,256]{2,1,0:T(8,128)S(1)}, f32[2,256,256]{2,1,0:T(8,128)S(1)}, u32[]{:S(2)}, u32[]{:S(2)}) collective-permute-start(f32[2,256,256]{2,1,0:T(8,128)S(1)} %maximum_select_fusion.5), channel_id=1, source_target_pairs={{0,2},{2,0},{4,6},{6,4},{8,10},{10,8},{12,14},{14,12},{16,18},{18,... | collective-permute-start | bytes 1572872 | tf_op jit(solution)/shard_map/ppermute | solution.py:16
  507.6 16.8 %copy-start.5 = (f32[256]{0:T(256)S(1)}, f32[256]{0:T(256)}, u32[]{:S(2)}) copy-start(f32[256]{0:T(256)} %param.14) | copy-start | bytes 3076
  507.6 16.8 %copy-start.6 = (f32[128]{0:T(128)S(1)}, f32[128]{0:T(128)}, u32[]{:S(2)}) copy-start(f32[128]{0:T(128)} %param.15) | copy-start | bytes 1540
Sparse Core Ops, SparseCore 0:
  511.3 13.0 reduce-scatter.1
where the time goes:
time: 543 us; the launch traced here: 533 us
  local copies, waits for them, and re-layouts  144 us (27%)
  waiting for transfers between devices  130 us (24%)
  other arithmetic  108 us (20%)
  matrix products  86 us (16%)
  starting transfers between devices  48.8 us (9%)
  between operations  14.2 us (3%)
    ppermute x7, waiting for transfers between devices, from_partner(): return lax.ppermute(value, axis, pairs)  98.6 us
    add x16, other arithmetic, dense_footprint(): dense + jnp.where(u_gap == tap_index, weights[tap_index][:, None], zero_v...  84.9 us
    dot_general x16, matrix products, accumulate(): lax.dot_general(u_dense, dense_v, (((0,), (0,)), ((), ())), preferred_ele...  54.1 us
    scatter x1, local copies, waits for them, and re-layouts, body(): jnp.zeros((4, slot_count), jnp.int32).at[:, target].set(descriptors)  47.4 us
    scatter x1, local copies, waits for them, and re-layouts, body(): jnp.zeros((2, slot_count), jnp.bfloat16).at[:, target].set(visibilities[0])  46.3 us
    all_to_all x1, starting transfers between devices, body(): lax.all_to_all(outgoing.reshape(2, img_count, capacity), 'img', split_axi...  29.1 us
    dot_general x16, matrix products, weighted_payload(): jnp.einsum('prk,kt->ptr', one_hot_taps, kernel, preferred_element_type=jn...  21 us
    all_to_all x1, waiting for transfers between devices, body(): lax.all_to_all(placing.reshape(4, img_count, capacity), 'img', split_axis...  18.6 us
  transfers between devices with their start and end apart: 10, of which 9 were waited for; matrix products, arithmetic and copies ran while one was open for 12% of the time, Pallas kernels for 0%

commit v1 on v0

v1 whole, which is shorter than its diff:
```python
import functools
import math

import jax
import jax.numpy as jnp
import numpy as np
from jax import lax
from jax.experimental import pallas as pl
from jax.experimental.pallas import tpu as pltpu
from jax.sharding import PartitionSpec as P

SUB = 256
TAPS = 8
OS = 128
IMG = 128
HALF = 128
CAP = 256
VIS = 16384
CHUNK = 2048
GROUP = 16
F32 = jnp.float32
BF16 = jnp.bfloat16
MESH = pl.DeviceIdType.MESH


def split_table(table):
    high = table.astype(np.float32).astype(jnp.bfloat16)
    low = (table - high.astype(np.float64)).astype(np.float32).astype(jnp.bfloat16)
    return np.stack([high, low])


def reversed_bits(count):
    bits = count.bit_length() - 1
    positions = np.arange(count)
    order = np.zeros(count, np.int64)
    for bit in range(bits):
        order |= (positions >> bit & 1) << bits - 1 - bit
    return order


@functools.lru_cache(maxsize=None)
def host_tables():
    points = np.arange(SUB)
    angle = 2 * np.pi * (points[:, None] * points[None, :] % SUB) / SUB
    cosine, sine = np.cos(angle), np.sin(angle)
    halves = [
        np.concatenate([cosine[:, h * HALF : (h + 1) * HALF], sine[:, h * HALF : (h + 1) * HALF]], 1)
        for h in (0, 1)
    ]
    v_tables = split_table(np.stack(halves))
    order = reversed_bits(IMG)
    places = np.arange(IMG)
    turn = 2 * np.pi * (order[:, None] * places[None, :] % IMG) / IMG
    across = np.stack([np.stack([np.cos(turn), -np.sin(turn)], -1), np.stack([np.sin(turn), np.cos(turn)], -1)], 1)
    u_table = np.einsum("apoq,hg->aphoqg", across, np.eye(2)).reshape(4 * IMG, 4 * IMG)
    u_tables = split_table(u_table)
    row = places[:, None, None] + np.zeros((1, 2, 1), np.int64) + IMG * np.arange(2)[None, None, :]
    quarter = np.zeros((IMG, 1, 1)) + np.arange(2)[None, :, None] + np.zeros((1, 1, 2))
    row, quarter = row.reshape(-1), quarter.reshape(-1)
    last = 2 * np.pi * (points[:, None] * row[None, :] % SUB) / SUB + quarter[None, :] * np.pi / 2
    last_tables = np.stack([np.cos(last), np.sin(last)]).astype(np.float32)
    twist = 2 * np.pi * (order[:, None] * row[None, :]) / (IMG * SUB)
    twists = np.stack([np.cos(twist), np.sin(twist)], 1).astype(np.float32)
    return v_tables, u_tables, last_tables, twists


def dot_nt(left, right):
    return lax.dot_general(left, right, (((1,), (1,)), ((), ())), preferred_element_type=F32)


def dot_nn(left, right):
    return lax.dot_general(left, right, (((1,), (0,)), ((), ())), preferred_element_type=F32)


def split_pair(value):
    high = value.astype(BF16)
    low = (value - high.astype(F32)).astype(BF16)
    return high, low


def bucket(vis_ref, own_ref, cells_ref, taps_ref, out_ref, acc, lhs, rhs):
    acc[...] = jnp.zeros_like(acc)
    first = lax.broadcasted_iota(jnp.int32, (SUB, SUB), 0)
    second = lax.broadcasted_iota(jnp.int32, (SUB, SUB), 1)
    upper = jnp.where(first <= second, 1.0, 0.0).astype(BF16)
    names = lax.broadcasted_iota(jnp.int32, (IMG, CHUNK), 0)
    lines = lax.broadcasted_iota(jnp.int32, (16, CHUNK), 0)
    lower_half = jnp.where(lines >= 8, 1.0, 0.0)
    lines = lines.astype(F32)
    zero = jnp.zeros((16, CHUNK), BF16)
    one = jnp.ones((16, CHUNK), BF16)

    def step(turn, carry):
        columns = pl.ds(pl.multiple_of(turn * CHUNK, CHUNK), CHUNK)
        owners = own_ref[:, columns]
        named = jnp.where(names == owners, 1.0, 0.0)
        marks = named.astype(BF16)
        ranks = []
        for part in range(CHUNK // SUB):
            span = slice(part * SUB, (part + 1) * SUB)
            counts = dot_nn(marks[:, span], upper) + carry
            ranks.append(jnp.sum(named[:, span] * counts, axis=0, keepdims=True) - 1.0)
            carry = counts[:, SUB - 1 : SUB]
        rank = jnp.concatenate(ranks, axis=1)
        gap = (rank - lines).astype(BF16)
        for block in range(CAP // 16):
            rhs[block * 16 : (block + 1) * 16, :] = jnp.where(gap == block * 16, one, zero)
        features = jnp.concatenate(
            [
                vis_ref[:, columns].astype(F32),
                cells_ref[:, columns].astype(F32),
                taps_ref[:, columns].astype(F32),
                jnp.zeros((2, CHUNK), F32),
            ],
            axis=0,
        )
        features = jnp.concatenate([features, features], axis=0).astype(BF16)
        owner_gap = (owners.astype(F32) - lower_half).astype(BF16)
        for block in range(IMG // 2):
            lhs[block * 16 : (block + 1) * 16, :] = jnp.where(owner_gap == 2 * block, features, zero)
        acc[...] += dot_nt(lhs[...], rhs[...])
        return carry

    lax.fori_loop(0, VIS // CHUNK, step, jnp.zeros((IMG, 1), F32))
    total = acc[...]
    front = total[:, :HALF].reshape(IMG, 8, HALF)
    back = total[:, HALF:].reshape(IMG, 8, HALF)
    out_ref[...] = jnp.concatenate([front, back], axis=1).astype(BF16)


def spread(table, cell, tap, lines):
    block = jnp.floor(cell * 0.125)
    low = cell - block * 8.0
    gap = lines - low
    wraps = gap < 0.0
    source = jnp.where(wraps, gap + 8.0, gap).astype(jnp.int32)
    looked = jnp.take_along_axis(table, tap.astype(jnp.int32), axis=1)
    turned = jnp.take_along_axis(looked, source, axis=0)
    return turned, block + jnp.where(wraps, 1.0, 0.0)


def grid_group(arrived, start, table, lhs, rhs):
    lines = lax.broadcasted_iota(jnp.int32, (8, HALF), 0).astype(F32)
    zero = jnp.zeros((16, HALF), BF16)
    for source in range(GROUP):
        message = arrived[start + source].astype(F32)
        for half in range(2):
            slots = message[half * 8 : half * 8 + 8]
            columns = slice((source * 2 + half) * HALF, (source * 2 + half + 1) * HALF)

            def line(index):
                return jnp.broadcast_to(slots[index : index + 1], (8, HALF))

            turned_u, block_u = spread(table, line(2), line(4), lines)
            turned_v, block_v = spread(table, line(3), line(5), lines)
            real, imag = line(0) * turned_u, line(1) * turned_u
            real = jnp.concatenate([real, real], axis=0).astype(BF16)
            imag = jnp.concatenate([imag, imag], axis=0).astype(BF16)
            weight_v = jnp.concatenate([turned_v, turned_v], axis=0).astype(BF16)
            at_u = jnp.concatenate([block_u, block_u - 1.0], axis=0).astype(BF16)
            at_v = jnp.concatenate([block_v, block_v - 1.0], axis=0).astype(BF16)
            for block in range(SUB // 16):
                here = at_u == 2 * block
                lhs[block * 16 : (block + 1) * 16, columns] = jnp.where(here, real, zero)
                lhs[SUB + block * 16 : SUB + (block + 1) * 16, columns] = jnp.where(here, imag, zero)
                rhs[block * 16 : (block + 1) * 16, columns] = jnp.where(at_v == 2 * block, weight_v, zero)


def main_kernel(
    vis_ref, own_ref, cells_ref, taps_ref, table_ref, rows_ref, cols_ref, v_ref, u_ref, last_ref, twist_ref, out_ref,
    big, lhs, rhs, lhs_grid, rhs_grid, sent, arrived, grid, cross_out, cross_in, out_two, in_two, out_three, in_three,
    final_table, factor, send_sem, recv_sem, cross_sem, far_send, far_recv, own_sem,
):
    me, chan = lax.axis_index("img"), lax.axis_index("chan")
    barrier = pltpu.get_barrier_semaphore()

    def greet(step, count):
        pl.semaphore_signal(barrier, inc=1, device_id=(lax.rem(me + step, IMG), chan), device_id_type=MESH)
        return count

    lax.fori_loop(1, IMG, greet, 0)
    pl.semaphore_signal(barrier, inc=1, device_id=(me, 1 - chan), device_id_type=MESH)

    bucket(vis_ref, own_ref, cells_ref, taps_ref, sent, big, lhs, rhs)

    pl.semaphore_wait(barrier, IMG)

    pltpu.make_async_copy(sent.at[me], arrived.at[0], own_sem.at[0]).start()

    def send_vis(step, count):
        peer = lax.rem(me + step, IMG)
        pltpu.make_async_remote_copy(
            src_ref=sent.at[peer], dst_ref=arrived.at[step], send_sem=send_sem,
            recv_sem=recv_sem.at[step // GROUP], device_id=(peer, chan), device_id_type=MESH,
        ).start()
        return count

    lax.fori_loop(1, IMG, send_vis, 0)

    cosine, sine = twist_ref[me, 0:1, :], twist_ref[me, 1:2, :]
    scale = 1.0 / math.sqrt(SUB * IMG * SUB)
    for block in range(2):
        rows = slice(block * HALF, (block + 1) * HALF)
        base_cos, base_sin = last_ref[0, rows, :], last_ref[1, rows, :]
        high, low = split_pair(base_cos * cosine - base_sin * sine)
        final_table[0, rows, :] = high
        final_table[1, rows, :] = low
        rows_low = slice(SUB + block * HALF, SUB + (block + 1) * HALF)
        high, low = split_pair(base_sin * cosine + base_cos * sine)
        final_table[0, rows_low, :] = high
        final_table[1, rows_low, :] = low
        column = jnp.transpose(jnp.broadcast_to(rows_ref[:, rows], (HALF, HALF)))
        factor[rows, :] = column * cols_ref[...] * scale

    grid[...] = jnp.zeros_like(grid)
    table = table_ref[...].astype(F32)

    def wait_span(count, semaphore):
        span = pl.ds(0, count)
        pltpu.make_async_remote_copy(
            src_ref=sent.at[span], dst_ref=arrived.at[span], send_sem=send_sem, recv_sem=semaphore,
            device_id=(me, 1 - chan), device_id_type=MESH,
        ).wait_recv()

    pltpu.make_async_copy(sent.at[me], arrived.at[0], own_sem.at[0]).wait()
    wait_span(GROUP - 1, recv_sem.at[0])

    def grid_step(group, count):
        @pl.when(group > 0)
        def _():
            wait_span(GROUP, recv_sem.at[group])

        grid_group(arrived, group * GROUP, table, lhs_grid, rhs_grid)
        grid[...] += dot_nt(lhs_grid[...], rhs_grid[...])
        return count

    lax.fori_loop(0, IMG // GROUP, grid_step, 0)

    grid_high, grid_low = split_pair(grid[...])

    def half_spectrum(half):
        high, low = v_ref[0, half], v_ref[1, half]
        both = dot_nn(grid_high, high) + (dot_nn(grid_high, low) + dot_nn(grid_low, high))
        real = both[:SUB, :HALF] - both[SUB:, HALF:]
        imag = both[:SUB, HALF:] + both[SUB:, :HALF]
        return jnp.concatenate([real, imag], axis=0)

    cross_out[...] = half_spectrum(1 - chan)
    cross = pltpu.make_async_remote_copy(
        src_ref=cross_out, dst_ref=cross_in, send_sem=cross_sem.at[0], recv_sem=cross_sem.at[1],
        device_id=(me, 1 - chan), device_id_type=MESH,
    )
    cross.start()
    mine = half_spectrum(chan)
    place = lax.broadcasted_iota(jnp.int32, (4 * IMG, 4 * IMG), 0)
    origin = lax.broadcasted_iota(jnp.int32, (4 * IMG, 4 * IMG), 1)
    swap = jnp.where(origin == (place & 3) * IMG + (place >> 2), 1.0, 0.0).astype(BF16)
    cross.wait_recv()
    summed = (mine + cross_in[...]).astype(BF16)
    out_two[...] = dot_nn(swap, summed).reshape(IMG, 4, HALF).astype(BF16)

    def exchange(source, target, phase):
        keep = pltpu.make_async_copy(source.at[me], target.at[me], own_sem.at[1 + phase])
        keep.start()

        def send(step, count):
            peer = lax.rem(me + step, IMG)
            pltpu.make_async_remote_copy(
                src_ref=source.at[peer], dst_ref=target.at[me], send_sem=far_send.at[phase],
                recv_sem=far_recv.at[phase], device_id=(peer, chan), device_id_type=MESH,
            ).start()
            return count

        lax.fori_loop(1, IMG, send, 0)
        keep.wait()
        span = pl.ds(0, IMG - 1)
        return pltpu.make_async_remote_copy(
            src_ref=source.at[span], dst_ref=target.at[span], send_sem=far_send.at[phase],
            recv_sem=far_recv.at[phase], device_id=(me, 1 - chan), device_id_type=MESH,
        )

    second = exchange(out_two, in_two, 0)
    second.wait_recv()
    columns = in_two[...].reshape(4 * IMG, HALF)
    lines = dot_nn(u_ref[0], columns) + dot_nn(u_ref[1], columns)
    out_three[...] = lines.reshape(IMG, 4, HALF).astype(BF16)
    third = exchange(out_three, in_three, 1)
    third.wait_recv()
    columns = in_three[...].reshape(4 * IMG, HALF)
    image = dot_nn(final_table[0], columns) + dot_nn(final_table[1], columns)
    out_ref[0] = image[:SUB] * factor[...]
    out_ref[1] = image[SUB:] * factor[...]

    span = pl.ds(0, IMG - 1)
    pltpu.make_async_remote_copy(
        src_ref=sent.at[span], dst_ref=arrived.at[span], send_sem=send_sem, recv_sem=recv_sem.at[0],
        device_id=(me, 1 - chan), device_id_type=MESH,
    ).wait_send()
    cross.wait_send()
    second.wait_send()
    third.wait_send()


def body(visibilities, owner, cells, taps, kernel, taper_rows, taper_cols):
    v_tables, u_tables, last_tables, twists = host_tables()
    return pl.pallas_call(
        main_kernel,
        out_shape=jax.ShapeDtypeStruct((2, SUB, HALF), F32),
        in_specs=[pl.BlockSpec(memory_space=pltpu.VMEM)] * 11,
        out_specs=pl.BlockSpec(memory_space=pltpu.VMEM),
        scratch_shapes=[
            pltpu.VMEM((8 * IMG, CAP), F32),
            pltpu.VMEM((8 * IMG, CHUNK), BF16),
            pltpu.VMEM((CAP, CHUNK), BF16),
            pltpu.VMEM((2 * SUB, GROUP * CAP), BF16),
            pltpu.VMEM((SUB, GROUP * CAP), BF16),
            pltpu.VMEM((IMG, 16, HALF), BF16),
            pltpu.VMEM((IMG, 16, HALF), BF16),
            pltpu.VMEM((2 * SUB, SUB), F32),
            pltpu.VMEM((2 * SUB, HALF), F32),
            pltpu.VMEM((2 * SUB, HALF), F32),
            pltpu.VMEM((IMG, 4, HALF), BF16),
            pltpu.VMEM((IMG, 4, HALF), BF16),
            pltpu.VMEM((IMG, 4, HALF), BF16),
            pltpu.VMEM((IMG, 4, HALF), BF16),
            pltpu.VMEM((2, 4 * IMG, 4 * IMG), BF16),
            pltpu.VMEM((SUB, HALF), F32),
            pltpu.SemaphoreType.DMA(()),
            pltpu.SemaphoreType.DMA((IMG // GROUP,)),
            pltpu.SemaphoreType.DMA((2,)),
            pltpu.SemaphoreType.DMA((2,)),
            pltpu.SemaphoreType.DMA((2,)),
            pltpu.SemaphoreType.DMA((3,)),
        ],
        compiler_params=pltpu.CompilerParams(
            collective_id=0, has_side_effects=True, vmem_limit_bytes=48 * 1024 * 1024
        ),
        name="gridding",
    )(
        visibilities[0], owner.reshape(1, VIS), cells[0], taps[0], kernel.T,
        taper_rows.reshape(1, SUB), taper_cols.reshape(1, HALF),
        jnp.asarray(v_tables), jnp.asarray(u_tables), jnp.asarray(last_tables), jnp.asarray(twists),
    )


def solution(mesh):
    return jax.shard_map(
        body,
        mesh=mesh,
        in_specs=(
            P("chan", None, "img"),
            P("chan", "img", None),
            P("chan", None, "img"),
            P("chan", None, "img"),
            P(),
            P("img"),
            P("chan"),
        ),
        out_specs=P(None, "img", "chan"),
        check_vma=False,
    )
```

time: 543 us -> 77 us (0.14); the launches traced: 533 us -> 76.7 us
  local copies, waits for them, and re-layouts: 144 us -> 9.41 us
  waiting for transfers between devices: 130 us -> 0 us
  other arithmetic: 108 us -> 0 us
  matrix products: 86 us -> 0 us
  Pallas kernels: 0 us -> 67.2 us
  starting transfers between devices: 48.8 us -> 0 us
  between operations: 14.2 us -> 0.02 us
    ppermute x7 -> x0, waiting for transfers between devices: 98.6 us -> none  [from_partner(): return lax.ppermute(value, axis, pairs)]
    scatter x2 -> x0, local copies, waits for them, and re-layouts: 93.6 us -> none  [the longest x1 47.4 us: body(): jnp.zeros((4, slot_count), jnp.int32).at[:, target].set(descriptors)]
    dot_general x40 -> x0, matrix products: 86 us -> none  [the longest x16 54.1 us: accumulate(): lax.dot_general(u_dense, dense_v, (((0,), (0,)), ((), ())), preferred_ele...]
    add x16 -> x0, other arithmetic: 84.9 us -> none  [dense_footprint(): dense + jnp.where(u_gap == tap_index, weights[tap_index][:, None], zero_v...]
    pallas_call x0 -> x1, Pallas kernels: none -> 67.2 us  [body(): pl.pallas_call(main_kernel, out_shape=jax.ShapeDtypeStruct((2, SUB, HALF)...]
    all_to_all x2 -> x0, starting transfers between devices: 42.3 us -> none  [the longest x1 29.1 us: body(): lax.all_to_all(outgoing.reshape(2, img_count, capacity), 'img', split_axi...]
    all_to_all x2 -> x0, waiting for transfers between devices: 18.6 us -> none  [the longest x1 18.6 us: body(): lax.all_to_all(placing.reshape(4, img_count, capacity), 'img', split_axis...]
    reshape x2 -> x0, local copies, waits for them, and re-layouts: 16.9 us -> none  [the longest x1 9.87 us: body(): placing.reshape(4, img_count, capacity)]
  transfers between devices with their start and end apart: 10 -> 0, of which waited for: 9 -> 0; matrix products, arithmetic and copies ran while one was open for 12% -> 0% of each run, Pallas kernels for 0% -> 0%
where the time goes in v1:
time: 77 us; the launch traced here: 76.7 us
  Pallas kernels  67.2 us (87%)
  local copies, waits for them, and re-layouts  9.41 us (12%)
    pallas_call x1, Pallas kernels, body(): pl.pallas_call(main_kernel, out_shape=jax.ShapeDtypeStruct((2, SUB, HALF)...  67.2 us
    unnamed x23, local copies, waits for them, and re-layouts  9.41 us

profile of v1, /device:TPU:1, one launch (start us, length us, event | category | flops | bytes accessed | tf_op | source)
XLA Modules:
  0.0 76.7 jit_solution(928602649703528140)
XLA Ops:
  0.0 0.0 copy-start.8
  0.0 0.0 copy-start.9
  0.0 0.0 copy-start.10
  0.0 0.7 copy-done.8
  0.7 0.0 copy-done.9
  0.7 0.0 copy-done.10
  0.7 0.0 copy-start
  0.7 1.2 %copy-done = f32[2,256,512]{2,1,0:T(8,128)S(1)} copy-done((f32[2,256,512]{2,1,0:T(8,128)S(1)}, f32[2,256,512]{2,1,0:T(8,128)}, u32[]{:S(2)}) %copy-start) | copy-done | bytes 1048600
  1.9 0.0 copy-start.1
  1.9 1.2 %copy-done.1 = bf16[2,512,512]{2,1,0:T(8,128)(2,1)S(1)} copy-done((bf16[2,512,512]{2,1,0:T(8,128)(2,1)S(1)}, bf16[2,512,512]{2,1,0:T(8,128)(2,1)}, u32[]{:S(2)}) %copy-start.1) | copy-done | bytes 1048600
  3.1 0.0 copy-start.2
  3.2 1.0 %copy-done.2 = f32[128,2,512]{2,1,0:T(2,128)S(1)} copy-done((f32[128,2,512]{2,1,0:T(2,128)S(1)}, f32[128,2,512]{2,1,0:T(2,128)}, u32[]{:S(2)}) %copy-start.2) | copy-done | bytes 524312
  4.2 0.0 copy-start.3
  4.2 1.0 %copy-done.3 = bf16[2,2,256,256]{3,2,1,0:T(8,128)(2,1)S(1)} copy-done((bf16[2,2,256,256]{3,2,1,0:T(8,128)(2,1)S(1)}, bf16[2,2,256,256]{3,2,1,0:T(8,128)(2,1)}, u32[]{:S(2)}) %copy-start.3) | copy-done | bytes 524312
  5.2 0.0 copy-start.4
  5.2 0.9 %copy-done.4 = s32[1,2,16384]{2,1,0:T(2,128)S(1)} copy-done((s32[1,2,16384]{2,1,0:T(2,128)S(1)}, s32[1,2,16384]{2,1,0:T(2,128)}, u32[]{:S(2)}) %copy-start.4) | copy-done | bytes 131096
  6.1 0.0 copy-start.5
  6.1 0.9 %copy-done.5 = s32[1,2,16384]{2,1,0:T(2,128)S(1)} copy-done((s32[1,2,16384]{2,1,0:T(2,128)S(1)}, s32[1,2,16384]{2,1,0:T(2,128)}, u32[]{:S(2)}) %copy-start.5) | copy-done | bytes 131096
  7.0 0.0 copy-start.6
  7.0 0.8 %copy-done.6 = bf16[1,2,16384]{2,1,0:T(2,128)(2,1)S(1)} copy-done((bf16[1,2,16384]{2,1,0:T(2,128)(2,1)S(1)}, bf16[1,2,16384]{2,1,0:T(2,128)(2,1)}, u32[]{:S(2)}) %copy-start.6) | copy-done | bytes 65560
  7.9 0.0 copy-start.7
  7.9 0.8 %copy-done.7 = s32[1,16384,1]{1,2,0:T(1,128)S(1)} copy-done((s32[1,16384,1]{1,2,0:T(1,128)S(1)}, s32[1,16384,1]{1,2,0:T(1,128)}, u32[]{:S(2)}) %copy-start.7) | copy-done | bytes 65560
  8.7 67.2 %gridding.1 = f32[2,256,128]{2,1,0:T(8,128)S(1)} custom-call(bf16[2,16384]{1,0:T(2,128)(2,1)S(1)} %bitcast.9, s32[1,16384]{1,0:T(1,128)S(1)} %bitcast.10, s32[2,16384]{1,0:T(2,128)S(1)} %bitcast.7, s32[2,16384]{1,0:T(2,128)S(1)} %bitcast.8, bf16[8,128]{1,0:T(8,128)(2,1)S(1)} %bitcast.11, f32[1,256]{1,0:T(1,128)S(1)} %bitcast.12, f32[1,128]{1,0:T(1,128)S(1)} %bitcast.13, ...), custom_call_target="tpu_custom_call" | custom-call | tf_op jit(solution)/shard_map/gridding/pallas_call | solution.py:306
  75.9 0.7 copy.13
Async XLA Ops:
  0.0 0.7 copy-start.8
  0.0 0.7 copy-start.9
  0.0 0.7 copy-start.10
  0.7 1.2 %copy-start = (f32[2,256,512]{2,1,0:T(8,128)S(1)}, f32[2,256,512]{2,1,0:T(8,128)}, u32[]{:S(2)}) copy-start(f32[2,256,512]{2,1,0:T(8,128)} %constant.10.clone.last_ref) | copy-start | bytes 3145732
  1.9 1.2 %copy-start.1 = (bf16[2,512,512]{2,1,0:T(8,128)(2,1)S(1)}, bf16[2,512,512]{2,1,0:T(8,128)(2,1)}, u32[]{:S(2)}) copy-start(bf16[2,512,512]{2,1,0:T(8,128)(2,1)} %constant.9.clone.u_ref) | copy-start | bytes 3145732
  3.1 1.0 %copy-start.2 = (f32[128,2,512]{2,1,0:T(2,128)S(1)}, f32[128,2,512]{2,1,0:T(2,128)}, u32[]{:S(2)}) copy-start(f32[128,2,512]{2,1,0:T(2,128)} %constant.11.clone.twist_ref) | copy-start | bytes 1572868
  4.2 1.0 %copy-start.3 = (bf16[2,2,256,256]{3,2,1,0:T(8,128)(2,1)S(1)}, bf16[2,2,256,256]{3,2,1,0:T(8,128)(2,1)}, u32[]{:S(2)}) copy-start(bf16[2,2,256,256]{3,2,1,0:T(8,128)(2,1)} %constant.8.clone.v_ref) | copy-start | bytes 1572868
  5.2 0.9 %copy-start.4 = (s32[1,2,16384]{2,1,0:T(2,128)S(1)}, s32[1,2,16384]{2,1,0:T(2,128)}, u32[]{:S(2)}) copy-start(s32[1,2,16384]{2,1,0:T(2,128)} %param.13) | copy-start | bytes 393220
  6.1 0.9 %copy-start.5 = (s32[1,2,16384]{2,1,0:T(2,128)S(1)}, s32[1,2,16384]{2,1,0:T(2,128)}, u32[]{:S(2)}) copy-start(s32[1,2,16384]{2,1,0:T(2,128)} %param.14) | copy-start | bytes 393220
  7.0 0.8 %copy-start.6 = (bf16[1,2,16384]{2,1,0:T(2,128)(2,1)S(1)}, bf16[1,2,16384]{2,1,0:T(2,128)(2,1)}, u32[]{:S(2)}) copy-start(bf16[1,2,16384]{2,1,0:T(2,128)(2,1)} %param.11) | copy-start | bytes 196612
  7.9 0.8 %copy-start.7 = (s32[1,16384,1]{1,2,0:T(1,128)S(1)}, s32[1,16384,1]{1,2,0:T(1,128)}, u32[]{:S(2)}) copy-start(s32[1,16384,1]{1,2,0:T(1,128)} %param.12) | copy-start | bytes 196612

commit v2 on v1

v2 whole, which is shorter than its diff:
```python
import functools
import math

import jax
import jax.numpy as jnp
import numpy as np
from jax import lax
from jax.experimental import pallas as pl
from jax.experimental.pallas import tpu as pltpu
from jax.sharding import PartitionSpec as P

SUB = 256
TAPS = 8
OS = 128
IMG = 128
HALF = 128
CAP = 256
VIS = 16384
CHUNK = 4096
BLOCK = 16
GROUP = 32
ORDER = (0, 7, 1, 6, 2, 5, 3, 4)
FAR = 72
F32 = jnp.float32
BF16 = jnp.bfloat16
MESH = pl.DeviceIdType.MESH


def split_table(table):
    high = table.astype(np.float32).astype(jnp.bfloat16)
    low = (table - high.astype(np.float64)).astype(np.float32).astype(jnp.bfloat16)
    return high, low


def reversed_bits(count):
    bits = count.bit_length() - 1
    positions = np.arange(count)
    order = np.zeros(count, np.int64)
    for bit in range(bits):
        order |= (positions >> bit & 1) << bits - 1 - bit
    return order


@functools.lru_cache(maxsize=None)
def host_tables():
    points = np.arange(SUB)
    angle = 2 * np.pi * (points[:, None] * points[None, :] % SUB) / SUB
    cosine, sine = np.cos(angle), np.sin(angle)
    halves = []
    for start in (0, HALF):
        half_cos, half_sin = cosine[:, start : start + HALF], sine[:, start : start + HALF]
        high, low = split_table(np.block([[half_cos, half_sin], [-half_sin, half_cos]]))
        halves.append(np.concatenate([high, low, high], axis=0))
    v_tables = np.stack(halves)
    order = reversed_bits(IMG)
    turn = 2 * np.pi * (order[:, None] * np.arange(IMG)[None, :] % IMG) / IMG
    each = np.eye(2)
    high, low = split_table(np.concatenate([np.kron(np.cos(turn), each), np.kron(np.sin(turn), each)], axis=0))
    u_table = np.concatenate([high, low], axis=1)
    last_tables = np.stack([cosine, sine]).astype(np.float32)
    twist = 2 * np.pi * (order[:, None] * points[None, :]) / (IMG * SUB)
    twists = np.stack([np.cos(twist), np.sin(twist)], 1).astype(np.float32)
    return v_tables, u_table, last_tables, twists


def dot_nt(left, right):
    return lax.dot_general(left, right, (((1,), (1,)), ((), ())), preferred_element_type=F32)


def dot_nn(left, right):
    return lax.dot_general(left, right, (((1,), (0,)), ((), ())), preferred_element_type=F32)


def split_pair(value):
    high = value.astype(BF16)
    low = (value - high.astype(F32)).astype(BF16)
    return high, low


def encode(cell, tap):
    code = jnp.full(cell.shape, 2.0**-124, F32)
    for bit in range(7):
        code = jnp.where((cell >> bit & 1) == 1, code * 2.0 ** (1 << bit), code)
    code = jnp.where(cell >> 7 == 1, code * 2.0**64 * 2.0**64, code)
    return code * (1.0 + tap.astype(F32) * (1.0 / OS))


def decode(code):
    cell = jnp.zeros(code.shape, F32)
    large = code >= 2.0**4
    code = jnp.where(large, code * 2.0**-64 * 2.0**-64, code)
    cell = jnp.where(large, cell + 128.0, cell)
    for bit in range(6, -1, -1):
        large = code >= 2.0 ** ((1 << bit) - 124)
        code = jnp.where(large, code * 2.0 ** -(1 << bit), code)
        cell = jnp.where(large, cell + float(1 << bit), cell)
    tap = jnp.maximum((code * 2.0**124 - 1.0) * OS, 0.0)
    return cell, tap


def bucket(me, vis_ref, own_ref, cells_ref, taps_ref, lhs, rhs, acc):
    first = lax.broadcasted_iota(jnp.int32, (SUB, SUB), 0)
    second = lax.broadcasted_iota(jnp.int32, (SUB, SUB), 1)
    upper = jnp.where(first <= second, 1.0, 0.0).astype(BF16)
    names = lax.broadcasted_iota(jnp.int32, (IMG, CHUNK), 0)
    lines = lax.broadcasted_iota(jnp.int32, (16, CHUNK), 0).astype(F32)
    zero = jnp.zeros((16, CHUNK), BF16)
    one = jnp.ones((16, CHUNK), BF16)
    acc[...] = jnp.zeros_like(acc)

    def step(turn, carry):
        columns = pl.ds(pl.multiple_of(turn * CHUNK, CHUNK), CHUNK)
        offsets = (own_ref[:, columns] + (IMG - me)) & (IMG - 1)
        named = jnp.where(names == offsets, 1.0, 0.0)
        marks = named.astype(BF16)
        ranks = []
        for part in range(CHUNK // SUB):
            span = slice(part * SUB, (part + 1) * SUB)
            counts = dot_nn(marks[:, span], upper) + carry
            ranks.append(jnp.sum(named[:, span] * counts, axis=0, keepdims=True) - 1.0)
            carry = counts[:, SUB - 1 : SUB]
        rank = jnp.concatenate(ranks, axis=1)
        gap = (rank - lines).astype(BF16)
        for block in range(CAP // 16):
            rhs[block * 16 : (block + 1) * 16, :] = jnp.where(gap == block * 16, one, zero)
        codes = encode(cells_ref[:, columns], taps_ref[:, columns])
        features = [
            jnp.broadcast_to(row, (16, CHUNK)).astype(BF16)
            for row in (
                vis_ref[0:1, columns].astype(F32), vis_ref[1:2, columns].astype(F32), codes[0:1], codes[1:2],
            )
        ]
        offset_gap = (offsets.astype(F32) - lines).astype(BF16)
        for block, group in enumerate(ORDER):
            here = offset_gap == group * BLOCK
            for index, feature in enumerate(features):
                row = (block * 4 + index) * 16
                lhs[row : row + 16, :] = jnp.where(here, feature, zero)
        acc[...] += dot_nt(lhs[...], rhs[...])
        return carry

    lax.fori_loop(0, VIS // CHUNK, step, jnp.zeros((IMG, 1), F32))


def make_messages(block, acc, out_ref):
    place = lax.broadcasted_iota(jnp.int32, (8 * 16, 6 * 16), 0)
    origin = lax.broadcasted_iota(jnp.int32, (8 * 16, 6 * 16), 1)
    swap = jnp.where(origin == (place & 7) * 16 + (place >> 3), 1.0, 0.0).astype(BF16)
    found = acc[block * 64 : (block + 1) * 64, :]
    cell, tap = decode(found[32:])
    features = jnp.concatenate([found[:32], cell, tap], axis=0).astype(BF16)
    swapped = dot_nn(swap, features)
    front = swapped[:, :HALF].reshape(16, 8, HALF)
    back = swapped[:, HALF:].reshape(16, 8, HALF)
    out_ref[block * 16 : (block + 1) * 16] = jnp.concatenate([front, back], axis=1).astype(BF16)


def spread(table, cell, tap, lines):
    block = jnp.floor(cell * 0.125)
    low = cell - block * 8.0
    gap = lines - low
    wraps = gap < 0.0
    source = jnp.where(wraps, gap + 8.0, gap).astype(jnp.int32)
    looked = jnp.take_along_axis(table, tap.astype(jnp.int32), axis=1)
    turned = jnp.take_along_axis(looked, source, axis=0)
    return turned, block + jnp.where(wraps, 1.0, 0.0)


def grid_group(arrived, start, table, lhs, rhs):
    lines = lax.broadcasted_iota(jnp.int32, (8, HALF), 0).astype(F32)
    zero = jnp.zeros((16, HALF), BF16)
    for source in range(GROUP):
        message = arrived[start + source].astype(F32)
        for half in range(2):
            slots = message[half * 8 : half * 8 + 8]
            columns = slice((source * 2 + half) * HALF, (source * 2 + half + 1) * HALF)

            def line(index):
                return jnp.broadcast_to(slots[index : index + 1], (8, HALF))

            turned_u, block_u = spread(table, line(2), line(4), lines)
            turned_v, block_v = spread(table, line(3), line(5), lines)
            real, imag = line(0) * turned_u, line(1) * turned_u
            real = jnp.concatenate([real, real], axis=0).astype(BF16)
            imag = jnp.concatenate([imag, imag], axis=0).astype(BF16)
            weight_v = jnp.concatenate([turned_v, turned_v], axis=0).astype(BF16)
            at_u = jnp.concatenate([block_u, block_u - 1.0], axis=0).astype(BF16)
            at_v = jnp.concatenate([block_v, block_v - 1.0], axis=0).astype(BF16)
            for block in range(SUB // 16):
                here = at_u == 2 * block
                lhs[block * 16 : (block + 1) * 16, columns] = jnp.where(here, real, zero)
                lhs[SUB + block * 16 : SUB + (block + 1) * 16, columns] = jnp.where(here, imag, zero)
                rhs[block * 16 : (block + 1) * 16, columns] = jnp.where(at_v == 2 * block, weight_v, zero)


def main_kernel(
    vis_hbm, own_hbm, cells_hbm, taps_hbm, table_hbm, rows_hbm, cols_hbm, v_hbm, u_hbm, last_hbm, twist_hbm, out_ref,
    vis_ref, own_ref, cells_ref, taps_ref, table_ref, rows_ref, cols_ref, v_ref, u_ref, last_ref, twist_ref,
    acc, lhs, rhs, lhs_grid, rhs_grid, sent, arrived, grid, cross_out, cross_in, out_two, in_two, out_three, in_three,
    final_table, factor, load_sem, send_sem, recv_sem, cross_sem, far_send, far_recv, own_sem,
):
    me, chan = lax.axis_index("img"), lax.axis_index("chan")
    loads = [
        pltpu.make_async_copy(source, target, load_sem.at[index])
        for index, (source, target) in enumerate(
            [
                (vis_hbm, vis_ref), (own_hbm, own_ref), (cells_hbm, cells_ref), (taps_hbm, taps_ref),
                (table_hbm, table_ref), (rows_hbm, rows_ref), (cols_hbm, cols_ref), (twist_hbm.at[me], twist_ref),
                (last_hbm, last_ref), (v_hbm, v_ref), (u_hbm, u_ref),
            ]
        )
    ]
    for load in loads:
        load.start()
    barrier = pltpu.get_barrier_semaphore()

    def greet(step, count):
        pl.semaphore_signal(barrier, inc=1, device_id=(lax.rem(me + step, IMG), chan), device_id_type=MESH)
        return count

    lax.fori_loop(1, IMG, greet, 0)
    pl.semaphore_signal(barrier, inc=1, device_id=(me, 1 - chan), device_id_type=MESH)

    for load in loads[:4]:
        load.wait()
    bucket(me, vis_ref, own_ref, cells_ref, taps_ref, lhs, rhs, acc)

    def send_block(block):
        group = ORDER[block]

        def send(step, count):
            peer = lax.rem(me + group * BLOCK + step, IMG)
            pltpu.make_async_remote_copy(
                src_ref=sent.at[block * BLOCK + step], dst_ref=arrived.at[block * BLOCK + step],
                send_sem=send_sem, recv_sem=recv_sem.at[block], device_id=(peer, chan), device_id_type=MESH,
            ).start()
            return count

        lax.fori_loop(0 if group else 1, BLOCK, send, 0)

    self_block = ORDER.index(0)
    own = pltpu.make_async_copy(sent.at[self_block * BLOCK], arrived.at[self_block * BLOCK], own_sem.at[0])
    make_messages(0, acc, sent)
    pl.semaphore_wait(barrier, IMG)
    own.start()
    send_block(0)
    for block in range(1, 8):
        make_messages(block, acc, sent)
        send_block(block)

    for load in loads[4:]:
        load.wait()
    cosine, sine = twist_ref[0:1, :], twist_ref[1:2, :]
    base_cos, base_sin = last_ref[0], last_ref[1]
    for part, value in enumerate((base_cos * cosine - base_sin * sine, base_sin * cosine + base_cos * sine)):
        high, low = split_pair(value)
        final_table[part * SUB : (part + 1) * SUB, :SUB] = high
        final_table[part * SUB : (part + 1) * SUB, SUB:] = low
    scale = 1.0 / math.sqrt(SUB * IMG * SUB)
    for block in range(2):
        rows = slice(block * HALF, (block + 1) * HALF)
        column = jnp.transpose(jnp.broadcast_to(rows_ref[:, rows], (HALF, HALF)))
        factor[rows, :] = column * cols_ref[...] * scale

    grid[...] = jnp.zeros_like(grid)
    table = table_ref[...].astype(F32)
    own.wait()

    def wait_block(block):
        def wait_count(count):
            span = pl.ds(0, count)
            pltpu.make_async_remote_copy(
                src_ref=sent.at[span], dst_ref=arrived.at[span], send_sem=send_sem, recv_sem=recv_sem.at[block],
                device_id=(me, 1 - chan), device_id_type=MESH,
            ).wait_recv()

        @pl.when(block == self_block)
        def _():
            wait_count(BLOCK - 1)

        @pl.when(block != self_block)
        def _():
            wait_count(BLOCK)

    def grid_step(group, count):
        for block in range(GROUP // BLOCK):
            wait_block(group * (GROUP // BLOCK) + block)
        grid_group(arrived, group * GROUP, table, lhs_grid, rhs_grid)
        grid[...] += dot_nt(lhs_grid[...], rhs_grid[...])
        return count

    lax.fori_loop(0, IMG // GROUP, grid_step, 0)

    both = jnp.concatenate([grid[:SUB, :], grid[SUB:, :]], axis=1)
    high, low = split_pair(both)
    pieces = jnp.concatenate([high, high, low], axis=1)

    cross_out[...] = dot_nn(pieces, v_ref[1 - chan])
    cross = pltpu.make_async_remote_copy(
        src_ref=cross_out, dst_ref=cross_in, send_sem=cross_sem.at[0], recv_sem=cross_sem.at[1],
        device_id=(me, 1 - chan), device_id_type=MESH,
    )
    cross.start()
    mine = dot_nn(pieces, v_ref[chan])
    cross.wait_recv()
    out_two[...] = (mine + cross_in[...]).reshape(IMG, 2, SUB).astype(BF16)

    def complex_dot(table, columns):
        product = dot_nn(table, jnp.concatenate([columns, columns], axis=0))
        real = product[:SUB, :HALF] - product[SUB:, HALF:]
        imag = product[SUB:, :HALF] + product[:SUB, HALF:]
        return real, imag

    def exchange(source, target, phase):
        keep = pltpu.make_async_copy(source.at[me], target.at[me], own_sem.at[1 + phase])
        keep.start()

        def send(step, count):
            peer = lax.rem(me + FAR + step, IMG)
            pltpu.make_async_remote_copy(
                src_ref=source.at[peer], dst_ref=target.at[me], send_sem=far_send.at[phase],
                recv_sem=far_recv.at[phase], device_id=(peer, chan), device_id_type=MESH,
            ).start()
            return count

        lax.fori_loop(0, IMG - FAR, send, 0)
        lax.fori_loop(IMG - FAR + 1, IMG, send, 0)
        keep.wait()
        span = pl.ds(0, IMG - 1)
        return pltpu.make_async_remote_copy(
            src_ref=source.at[span], dst_ref=target.at[span], send_sem=far_send.at[phase],
            recv_sem=far_recv.at[phase], device_id=(me, 1 - chan), device_id_type=MESH,
        )

    second = exchange(out_two, in_two, 0)
    second.wait_recv()
    real, imag = complex_dot(u_ref[...], in_two[...].reshape(SUB, SUB))
    out_three[...] = jnp.concatenate([real, imag], axis=1).reshape(IMG, 2, SUB).astype(BF16)
    third = exchange(out_three, in_three, 1)
    third.wait_recv()
    real, imag = complex_dot(final_table[...], in_three[...].reshape(SUB, SUB))
    out_ref[0] = real * factor[...]
    out_ref[1] = imag * factor[...]

    span = pl.ds(0, IMG - 1)
    pltpu.make_async_remote_copy(
        src_ref=sent.at[span], dst_ref=arrived.at[span], send_sem=send_sem, recv_sem=recv_sem.at[0],
        device_id=(me, 1 - chan), device_id_type=MESH,
    ).wait_send()
    cross.wait_send()
    second.wait_send()
    third.wait_send()


def body(visibilities, owner, cells, taps, kernel, taper_rows, taper_cols):
    v_tables, u_table, last_tables, twists = host_tables()
    return pl.pallas_call(
        main_kernel,
        out_shape=jax.ShapeDtypeStruct((2, SUB, HALF), F32),
        in_specs=[pl.BlockSpec(memory_space=pltpu.HBM)] * 11,
        out_specs=pl.BlockSpec(memory_space=pltpu.VMEM),
        scratch_shapes=[
            pltpu.VMEM((2, VIS), BF16),
            pltpu.VMEM((1, VIS), jnp.int32),
            pltpu.VMEM((2, VIS), jnp.int32),
            pltpu.VMEM((2, VIS), jnp.int32),
            pltpu.VMEM((TAPS, OS), BF16),
            pltpu.VMEM((1, SUB), F32),
            pltpu.VMEM((1, HALF), F32),
            pltpu.VMEM(v_tables.shape, BF16),
            pltpu.VMEM(u_table.shape, BF16),
            pltpu.VMEM(last_tables.shape, F32),
            pltpu.VMEM(twists.shape[1:], F32),
            pltpu.VMEM((4 * IMG, CAP), F32),
            pltpu.VMEM((4 * IMG, CHUNK), BF16),
            pltpu.VMEM((CAP, CHUNK), BF16),
            pltpu.VMEM((2 * SUB, GROUP * CAP), BF16),
            pltpu.VMEM((SUB, GROUP * CAP), BF16),
            pltpu.VMEM((IMG, 16, HALF), BF16),
            pltpu.VMEM((IMG, 16, HALF), BF16),
            pltpu.VMEM((2 * SUB, SUB), F32),
            pltpu.VMEM((SUB, SUB), F32),
            pltpu.VMEM((SUB, SUB), F32),
            pltpu.VMEM((IMG, 2, SUB), BF16),
            pltpu.VMEM((IMG, 2, SUB), BF16),
            pltpu.VMEM((IMG, 2, SUB), BF16),
            pltpu.VMEM((IMG, 2, SUB), BF16),
            pltpu.VMEM((2 * SUB, 2 * SUB), BF16),
            pltpu.VMEM((SUB, HALF), F32),
            pltpu.SemaphoreType.DMA((11,)),
            pltpu.SemaphoreType.DMA(()),
            pltpu.SemaphoreType.DMA((IMG // BLOCK,)),
            pltpu.SemaphoreType.DMA((2,)),
            pltpu.SemaphoreType.DMA((2,)),
            pltpu.SemaphoreType.DMA((2,)),
            pltpu.SemaphoreType.DMA((3,)),
        ],
        compiler_params=pltpu.CompilerParams(
            collective_id=0, has_side_effects=True, vmem_limit_bytes=60 * 1024 * 1024
        ),
        name="gridding",
    )(
        visibilities[0], owner.reshape(1, VIS), cells[0], taps[0], kernel.T,
        taper_rows.reshape(1, SUB), taper_cols.reshape(1, HALF),
        jnp.asarray(v_tables), jnp.asarray(u_table), jnp.asarray(last_tables), jnp.asarray(twists),
    )


def solution(mesh):
    return jax.shard_map(
        body,
        mesh=mesh,
        in_specs=(
            P("chan", None, "img"),
            P("chan", "img", None),
            P("chan", None, "img"),
            P("chan", None, "img"),
            P(),
            P("img"),
            P("chan"),
        ),
        out_specs=P(None, "img", "chan"),
        check_vma=False,
    )
```

time: 77 us -> 63.4 us (0.82)
  local copies, waits for them, and re-layouts: 9.41 us -> 1.67 us
  Pallas kernels: 67.2 us -> 61.6 us
    unnamed x23 -> x1, local copies, waits for them, and re-layouts: 9.41 us -> 1.67 us
    pallas_call x1, Pallas kernels: 67.2 us -> 61.6 us  [body(): pl.pallas_call(main_kernel, out_shape=jax.ShapeDtypeStruct((2, SUB, HALF)...]
where the time goes in v2:
time: 63.4 us; the launch traced here: 63.3 us
  Pallas kernels  61.6 us (97%)
  local copies, waits for them, and re-layouts  1.67 us (3%)
    pallas_call x1, Pallas kernels, body(): pl.pallas_call(main_kernel, out_shape=jax.ShapeDtypeStruct((2, SUB, HALF)...  61.6 us
    unnamed x1, local copies, waits for them, and re-layouts  1.67 us

profile of v2, /device:TPU:1, one launch (start us, length us, event | category | flops | bytes accessed | tf_op | source)
XLA Modules:
  0.0 63.3 jit_solution(15356205656132352921)
XLA Ops:
  0.0 61.6 %gridding.1 = f32[2,256,128]{2,1,0:T(8,128)} custom-call(bf16[2,16384]{1,0:T(2,128)(2,1)} %bitcast.9, s32[1,16384]{1,0:T(1,128)} %bitcast.10, s32[2,16384]{1,0:T(2,128)} %bitcast.7, s32[2,16384]{1,0:T(2,128)} %bitcast.8, bf16[8,128]{1,0:T(8,128)(2,1)} %bitcast.11, f32[1,256]{1,0:T(1,128)} %bitcast.12, f32[1,128]{1,0:T(1,128)} %bitcast.13, ...), custom_call_target="tpu_custom_call" | custom-call | tf_op jit(solution)/shard_map/gridding/pallas_call | solution.py:357
  61.6 1.7 %copy.13 = f32[2,256,128]{2,1,0:T(8,128)} copy(f32[2,256,128]{2,1,0:T(8,128)} %gridding.1) | data formatting | bytes 524288

commit v3 on v2

--- a/solution.py
+++ b/solution.py
@@ -16,14 +16,21 @@
 HALF = 128
 CAP = 256
 VIS = 16384
-CHUNK = 4096
+CHUNK = 8192
 BLOCK = 16
 GROUP = 32
 ORDER = (0, 7, 1, 6, 2, 5, 3, 4)
-FAR = 72
 F32 = jnp.float32
 BF16 = jnp.bfloat16
 MESH = pl.DeviceIdType.MESH
+
+
+def hops(offset):
+    return sum(min(step, size - step) for step, size in zip(offset, TORUS))
+
+
+TORUS = (4, 4, 8)
+FAR_FIRST = sorted(list(np.ndindex(TORUS))[1:], key=hops, reverse=True)
 
 
 def split_table(table):
@@ -102,27 +109,14 @@
     first = lax.broadcasted_iota(jnp.int32, (SUB, SUB), 0)
     second = lax.broadcasted_iota(jnp.int32, (SUB, SUB), 1)
     upper = jnp.where(first <= second, 1.0, 0.0).astype(BF16)
-    names = lax.broadcasted_iota(jnp.int32, (IMG, CHUNK), 0)
     lines = lax.broadcasted_iota(jnp.int32, (16, CHUNK), 0).astype(F32)
     zero = jnp.zeros((16, CHUNK), BF16)
     one = jnp.ones((16, CHUNK), BF16)
     acc[...] = jnp.zeros_like(acc)
 
     def step(turn, carry):
-        columns = pl.ds(pl.multiple_of(turn * CHUNK, CHUNK), CHUNK)
+        columns = slice(turn * CHUNK, (turn + 1) * CHUNK)
         offsets = (own_ref[:, columns] + (IMG - me)) & (IMG - 1)
-        named = jnp.where(names == offsets, 1.0, 0.0)
-        marks = named.astype(BF16)
-        ranks = []
-        for part in range(CHUNK // SUB):
-            span = slice(part * SUB, (part + 1) * SUB)
-            counts = dot_nn(marks[:, span], upper) + carry
-            ranks.append(jnp.sum(named[:, span] * counts, axis=0, keepdims=True) - 1.0)
-            carry = counts[:, SUB - 1 : SUB]
-        rank = jnp.concatenate(ranks, axis=1)
-        gap = (rank - lines).astype(BF16)
-        for block in range(CAP // 16):
-            rhs[block * 16 : (block + 1) * 16, :] = jnp.where(gap == block * 16, one, zero)
         codes = encode(cells_ref[:, columns], taps_ref[:, columns])
         features = [
             jnp.broadcast_to(row, (16, CHUNK)).astype(BF16)
@@ -131,15 +125,34 @@
             )
         ]
         offset_gap = (offsets.astype(F32) - lines).astype(BF16)
+        marks = []
         for block, group in enumerate(ORDER):
             here = offset_gap == group * BLOCK
+            marks.append(jnp.where(here, one, zero))
             for index, feature in enumerate(features):
                 row = (block * 4 + index) * 16
                 lhs[row : row + 16, :] = jnp.where(here, feature, zero)
+        marks = jnp.concatenate(marks, axis=0)
+        parts = [marks[:, part * SUB : (part + 1) * SUB] for part in range(CHUNK // SUB)]
+        within = dot_nn(jnp.concatenate(parts, axis=0), upper)
+        ranks = []
+        for index, part in enumerate(parts):
+            counts = within[index * IMG : (index + 1) * IMG] + carry
+            found = part * counts.astype(BF16)
+            while found.shape[0] > 16:
+                found = found[: found.shape[0] // 2] + found[found.shape[0] // 2 :]
+            ranks.append(jnp.sum(found.astype(F32), axis=0, keepdims=True) - 1.0)
+            carry = counts[:, SUB - 1 : SUB]
+        rank = jnp.concatenate(ranks, axis=1)
+        gap = (rank - lines).astype(BF16)
+        for block in range(CAP // 16):
+            rhs[block * 16 : (block + 1) * 16, :] = jnp.where(gap == block * 16, one, zero)
         acc[...] += dot_nt(lhs[...], rhs[...])
         return carry
 
-    lax.fori_loop(0, VIS // CHUNK, step, jnp.zeros((IMG, 1), F32))
+    carry = jnp.zeros((IMG, 1), F32)
+    for turn in range(VIS // CHUNK):
+        carry = step(turn, carry)
 
 
 def make_messages(block, acc, out_ref):
@@ -210,33 +223,33 @@
             ]
         )
     ]
-    for load in loads:
+    for load in loads[:4]:
         load.start()
     barrier = pltpu.get_barrier_semaphore()
 
-    def greet(step, count):
-        pl.semaphore_signal(barrier, inc=1, device_id=(lax.rem(me + step, IMG), chan), device_id_type=MESH)
-        return count
-
-    lax.fori_loop(1, IMG, greet, 0)
+    def greet(step):
+        pl.semaphore_signal(barrier, inc=1, device_id=((me + step) & (IMG - 1), chan), device_id_type=MESH)
+
     pl.semaphore_signal(barrier, inc=1, device_id=(me, 1 - chan), device_id_type=MESH)
-
+    for step in range(1, IMG // 2):
+        greet(step)
     for load in loads[:4]:
         load.wait()
+    for load in loads[4:]:
+        load.start()
+    for step in range(IMG // 2, IMG):
+        greet(step)
     bucket(me, vis_ref, own_ref, cells_ref, taps_ref, lhs, rhs, acc)
 
     def send_block(block):
-        group = ORDER[block]
-
-        def send(step, count):
-            peer = lax.rem(me + group * BLOCK + step, IMG)
-            pltpu.make_async_remote_copy(
-                src_ref=sent.at[block * BLOCK + step], dst_ref=arrived.at[block * BLOCK + step],
-                send_sem=send_sem, recv_sem=recv_sem.at[block], device_id=(peer, chan), device_id_type=MESH,
-            ).start()
-            return count
-
-        lax.fori_loop(0 if group else 1, BLOCK, send, 0)
+        for step in range(BLOCK):
+            offset = ORDER[block] * BLOCK + step
+            if offset:
+                pltpu.make_async_remote_copy(
+                    src_ref=sent.at[block * BLOCK + step], dst_ref=arrived.at[block * BLOCK + step],
+                    send_sem=send_sem, recv_sem=recv_sem.at[block],
+                    device_id=((me + offset) & (IMG - 1), chan), device_id_type=MESH,
+                ).start()
 
     self_block = ORDER.index(0)
     own = pltpu.make_async_copy(sent.at[self_block * BLOCK], arrived.at[self_block * BLOCK], own_sem.at[0])
@@ -250,6 +263,78 @@
 
     for load in loads[4:]:
         load.wait()
+    grid[...] = jnp.zeros_like(grid)
+    table = table_ref[...].astype(F32)
+    own.wait()
+
+    def wait_block(block):
+        def wait_count(count):
+            span = pl.ds(0, count)
+            pltpu.make_async_remote_copy(
+                src_ref=sent.at[span], dst_ref=arrived.at[span], send_sem=send_sem, recv_sem=recv_sem.at[block],
+                device_id=(me, 1 - chan), device_id_type=MESH,
+            ).wait_recv()
+
+        @pl.when(block == self_block)
+        def _():
+            wait_count(BLOCK - 1)
+
+        @pl.when(block != self_block)
+        def _():
+            wait_count(BLOCK)
+
+    def grid_step(group, count):
+        for block in range(GROUP // BLOCK):
+            wait_block(group * (GROUP // BLOCK) + block)
+        grid_group(arrived, group * GROUP, table, lhs_grid, rhs_grid)
+        grid[...] += dot_nt(lhs_grid[...], rhs_grid[...])
+        return count
+
+    lax.fori_loop(0, IMG // GROUP, grid_step, 0)
+
+    both = jnp.concatenate([grid[:SUB, :], grid[SUB:, :]], axis=1)
+    high, low = split_pair(both)
+    pieces = jnp.concatenate([high, high, low], axis=1)
+
+    cross_out[...] = dot_nn(pieces, v_ref[1 - chan])
+    cross = pltpu.make_async_remote_copy(
+        src_ref=cross_out, dst_ref=cross_in, send_sem=cross_sem.at[0], recv_sem=cross_sem.at[1],
+        device_id=(me, 1 - chan), device_id_type=MESH,
+    )
+    cross.start()
+    mine = dot_nn(pieces, v_ref[chan])
+    cross.wait_recv()
+    out_two[...] = (mine + cross_in[...]).reshape(IMG, 2, SUB).astype(BF16)
+
+    def complex_dot(table, columns):
+        product = dot_nn(table, jnp.concatenate([columns, columns], axis=0))
+        real = product[:SUB, :HALF] - product[SUB:, HALF:]
+        imag = product[SUB:, :HALF] + product[:SUB, HALF:]
+        return real, imag
+
+    place_y, place_x, place_z = me >> 5, me >> 3 & 3, me & 7
+    rows_y = [(place_y + step & 3) * 32 for step in range(TORUS[0])]
+    rows_x = [(place_x + step & 3) * 8 for step in range(TORUS[1])]
+    rows_z = [place_z + step & 7 for step in range(TORUS[2])]
+
+    def exchange(source, target, phase):
+        keep = pltpu.make_async_copy(source.at[me], target.at[me], own_sem.at[1 + phase])
+        keep.start()
+
+        for far_y, far_x, far_z in FAR_FIRST:
+            peer = rows_y[far_y] + rows_x[far_x] + rows_z[far_z]
+            pltpu.make_async_remote_copy(
+                src_ref=source.at[peer], dst_ref=target.at[me], send_sem=far_send.at[phase],
+                recv_sem=far_recv.at[phase], device_id=(peer, chan), device_id_type=MESH,
+            ).start()
+        keep.wait()
+        span = pl.ds(0, IMG - 1)
+        return pltpu.make_async_remote_copy(
+            src_ref=source.at[span], dst_ref=target.at[span], send_sem=far_send.at[phase],
+            recv_sem=far_recv.at[phase], device_id=(me, 1 - chan), device_id_type=MESH,
+        )
+
+    second = exchange(out_two, in_two, 0)
     cosine, sine = twist_ref[0:1, :], twist_ref[1:2, :]
     base_cos, base_sin = last_ref[0], last_ref[1]
     for part, value in enumerate((base_cos * cosine - base_sin * sine, base_sin * cosine + base_cos * sine)):
@@ -261,78 +346,6 @@
         rows = slice(block * HALF, (block + 1) * HALF)
         column = jnp.transpose(jnp.broadcast_to(rows_ref[:, rows], (HALF, HALF)))
         factor[rows, :] = column * cols_ref[...] * scale
-
-    grid[...] = jnp.zeros_like(grid)
-    table = table_ref[...].astype(F32)
-    own.wait()
-
-    def wait_block(block):
-        def wait_count(count):
-            span = pl.ds(0, count)
-            pltpu.make_async_remote_copy(
-                src_ref=sent.at[span], dst_ref=arrived.at[span], send_sem=send_sem, recv_sem=recv_sem.at[block],
-                device_id=(me, 1 - chan), device_id_type=MESH,
-            ).wait_recv()
-
-        @pl.when(block == self_block)
-        def _():
-            wait_count(BLOCK - 1)
-
-        @pl.when(block != self_block)
-        def _():
-            wait_count(BLOCK)
-
-    def grid_step(group, count):
-        for block in range(GROUP // BLOCK):
-            wait_block(group * (GROUP // BLOCK) + block)
-        grid_group(arrived, group * GROUP, table, lhs_grid, rhs_grid)
-        grid[...] += dot_nt(lhs_grid[...], rhs_grid[...])
-        return count
-
-    lax.fori_loop(0, IMG // GROUP, grid_step, 0)
-
-    both = jnp.concatenate([grid[:SUB, :], grid[SUB:, :]], axis=1)
-    high, low = split_pair(both)
-    pieces = jnp.concatenate([high, high, low], axis=1)
-
-    cross_out[...] = dot_nn(pieces, v_ref[1 - chan])
-    cross = pltpu.make_async_remote_copy(
-        src_ref=cross_out, dst_ref=cross_in, send_sem=cross_sem.at[0], recv_sem=cross_sem.at[1],
-        device_id=(me, 1 - chan), device_id_type=MESH,
-    )
-    cross.start()
-    mine = dot_nn(pieces, v_ref[chan])
-    cross.wait_recv()
-    out_two[...] = (mine + cross_in[...]).reshape(IMG, 2, SUB).astype(BF16)
-
-    def complex_dot(table, columns):
-        product = dot_nn(table, jnp.concatenate([columns, columns], axis=0))
-        real = product[:SUB, :HALF] - product[SUB:, HALF:]
-        imag = product[SUB:, :HALF] + product[:SUB, HALF:]
-        return real, imag
-
-    def exchange(source, target, phase):
-        keep = pltpu.make_async_copy(source.at[me], target.at[me], own_sem.at[1 + phase])
-        keep.start()
-
-        def send(step, count):
-            peer = lax.rem(me + FAR + step, IMG)
-            pltpu.make_async_remote_copy(
-                src_ref=source.at[peer], dst_ref=target.at[me], send_sem=far_send.at[phase],
-                recv_sem=far_recv.at[phase], device_id=(peer, chan), device_id_type=MESH,
-            ).start()
-            return count
-
-        lax.fori_loop(0, IMG - FAR, send, 0)
-        lax.fori_loop(IMG - FAR + 1, IMG, send, 0)
-        keep.wait()
-        span = pl.ds(0, IMG - 1)
-        return pltpu.make_async_remote_copy(
-            src_ref=source.at[span], dst_ref=target.at[span], send_sem=far_send.at[phase],
-            recv_sem=far_recv.at[phase], device_id=(me, 1 - chan), device_id_type=MESH,
-        )
-
-    second = exchange(out_two, in_two, 0)
     second.wait_recv()
     real, imag = complex_dot(u_ref[...], in_two[...].reshape(SUB, SUB))
     out_three[...] = jnp.concatenate([real, imag], axis=1).reshape(IMG, 2, SUB).astype(BF16)

time: 63.4 us -> 61.7 us (0.973)
  Pallas kernels: 61.6 us -> 59.9 us
    pallas_call x1, Pallas kernels: 61.6 us -> 59.9 us  [body(): pl.pallas_call(main_kernel, out_shape=jax.ShapeDtypeStruct((2, SUB, HALF)...]
where the time goes in v3:
time: 61.7 us; the launch traced here: 61.6 us
  Pallas kernels  59.9 us (97%)
  local copies, waits for them, and re-layouts  1.67 us (3%)
    pallas_call x1, Pallas kernels, body(): pl.pallas_call(main_kernel, out_shape=jax.ShapeDtypeStruct((2, SUB, HALF)...  59.9 us
    unnamed x1, local copies, waits for them, and re-layouts  1.67 us

profile of v3, /device:TPU:1, one launch (start us, length us, event | category | flops | bytes accessed | tf_op | source)
XLA Modules:
  0.0 61.6 jit_solution(6033582296242625211)
XLA Ops:
  0.0 59.9 %gridding.1 = f32[2,256,128]{2,1,0:T(8,128)} custom-call(bf16[2,16384]{1,0:T(2,128)(2,1)} %bitcast.9, s32[1,16384]{1,0:T(1,128)} %bitcast.10, s32[2,16384]{1,0:T(2,128)} %bitcast.7, s32[2,16384]{1,0:T(2,128)} %bitcast.8, bf16[8,128]{1,0:T(8,128)(2,1)} %bitcast.11, f32[1,256]{1,0:T(1,128)} %bitcast.12, f32[1,128]{1,0:T(1,128)} %bitcast.13, ...), custom_call_target="tpu_custom_call" | custom-call | tf_op jit(solution)/shard_map/gridding/pallas_call | solution.py:370
  59.9 1.7 %copy.13 = f32[2,256,128]{2,1,0:T(8,128)} copy(f32[2,256,128]{2,1,0:T(8,128)} %gridding.1) | data formatting | bytes 524288

commit v4 on v3

--- a/solution.py
+++ b/solution.py
@@ -16,7 +16,7 @@
 HALF = 128
 CAP = 256
 VIS = 16384
-CHUNK = 8192
+CHUNK = VIS
 BLOCK = 16
 GROUP = 32
 ORDER = (0, 7, 1, 6, 2, 5, 3, 4)
@@ -179,10 +179,10 @@
     return turned, block + jnp.where(wraps, 1.0, 0.0)
 
 
-def grid_group(arrived, start, table, lhs, rhs):
+def grid_group(arrived, start, count, table, lhs, rhs):
     lines = lax.broadcasted_iota(jnp.int32, (8, HALF), 0).astype(F32)
     zero = jnp.zeros((16, HALF), BF16)
-    for source in range(GROUP):
+    for source in range(count):
         message = arrived[start + source].astype(F32)
         for half in range(2):
             slots = message[half * 8 : half * 8 + 8]
@@ -209,7 +209,7 @@
 def main_kernel(
     vis_hbm, own_hbm, cells_hbm, taps_hbm, table_hbm, rows_hbm, cols_hbm, v_hbm, u_hbm, last_hbm, twist_hbm, out_ref,
     vis_ref, own_ref, cells_ref, taps_ref, table_ref, rows_ref, cols_ref, v_ref, u_ref, last_ref, twist_ref,
-    acc, lhs, rhs, lhs_grid, rhs_grid, sent, arrived, grid, cross_out, cross_in, out_two, in_two, out_three, in_three,
+    acc, lhs, rhs, sent, arrived, grid, cross_out, cross_in, out_two, in_two, out_three, in_three,
     final_table, factor, load_sem, send_sem, recv_sem, cross_sem, far_send, far_recv, own_sem,
 ):
     me, chan = lax.axis_index("img"), lax.axis_index("chan")
@@ -227,18 +227,19 @@
         load.start()
     barrier = pltpu.get_barrier_semaphore()
 
-    def greet(step):
-        pl.semaphore_signal(barrier, inc=1, device_id=((me + step) & (IMG - 1), chan), device_id_type=MESH)
-
+    place_y, place_x, place_z = me >> 5, me >> 3 & 3, me & 7
+    rows_y = [(place_y + step & 3) * 32 for step in range(TORUS[0])]
+    rows_x = [(place_x + step & 3) * 8 for step in range(TORUS[1])]
+    rows_z = [place_z + step & 7 for step in range(TORUS[2])]
+
+    for far_y, far_x, far_z in FAR_FIRST:
+        peer = rows_y[far_y] + rows_x[far_x] + rows_z[far_z]
+        pl.semaphore_signal(barrier, inc=1, device_id=(peer, chan), device_id_type=MESH)
     pl.semaphore_signal(barrier, inc=1, device_id=(me, 1 - chan), device_id_type=MESH)
-    for step in range(1, IMG // 2):
-        greet(step)
     for load in loads[:4]:
         load.wait()
     for load in loads[4:]:
         load.start()
-    for step in range(IMG // 2, IMG):
-        greet(step)
     bucket(me, vis_ref, own_ref, cells_ref, taps_ref, lhs, rhs, acc)
 
     def send_block(block):
@@ -283,11 +284,13 @@
         def _():
             wait_count(BLOCK)
 
+    columns = slice(0, GROUP * CAP)
+
     def grid_step(group, count):
         for block in range(GROUP // BLOCK):
             wait_block(group * (GROUP // BLOCK) + block)
-        grid_group(arrived, group * GROUP, table, lhs_grid, rhs_grid)
-        grid[...] += dot_nt(lhs_grid[...], rhs_grid[...])
+        grid_group(arrived, group * GROUP, GROUP, table, lhs, rhs)
+        grid[...] += dot_nt(lhs[:, columns], rhs[:, columns])
         return count
 
     lax.fori_loop(0, IMG // GROUP, grid_step, 0)
@@ -311,11 +314,6 @@
         real = product[:SUB, :HALF] - product[SUB:, HALF:]
         imag = product[SUB:, :HALF] + product[:SUB, HALF:]
         return real, imag
-
-    place_y, place_x, place_z = me >> 5, me >> 3 & 3, me & 7
-    rows_y = [(place_y + step & 3) * 32 for step in range(TORUS[0])]
-    rows_x = [(place_x + step & 3) * 8 for step in range(TORUS[1])]
-    rows_z = [place_z + step & 7 for step in range(TORUS[2])]
 
     def exchange(source, target, phase):
         keep = pltpu.make_async_copy(source.at[me], target.at[me], own_sem.at[1 + phase])
@@ -387,8 +385,6 @@
             pltpu.VMEM((4 * IMG, CAP), F32),
             pltpu.VMEM((4 * IMG, CHUNK), BF16),
             pltpu.VMEM((CAP, CHUNK), BF16),
-            pltpu.VMEM((2 * SUB, GROUP * CAP), BF16),
-            pltpu.VMEM((SUB, GROUP * CAP), BF16),
             pltpu.VMEM((IMG, 16, HALF), BF16),
             pltpu.VMEM((IMG, 16, HALF), BF16),
             pltpu.VMEM((2 * SUB, SUB), F32),

time: 61.7 us -> 61 us (0.989)
  Pallas kernels: 59.9 us -> 59.2 us
    pallas_call x1, Pallas kernels: 59.9 us -> 59.2 us  [body(): pl.pallas_call(main_kernel, out_shape=jax.ShapeDtypeStruct((2, SUB, HALF)...]
where the time goes in v4:
time: 61 us; the launch traced here: 60.9 us
  Pallas kernels  59.2 us (97%)
  local copies, waits for them, and re-layouts  1.67 us (3%)
    pallas_call x1, Pallas kernels, body(): pl.pallas_call(main_kernel, out_shape=jax.ShapeDtypeStruct((2, SUB, HALF)...  59.2 us
    unnamed x1, local copies, waits for them, and re-layouts  1.67 us

profile of v4, /device:TPU:1, one launch (start us, length us, event | category | flops | bytes accessed | tf_op | source)
XLA Modules:
  0.0 60.9 jit_solution(16395810805084059089)
XLA Ops:
  0.0 59.2 %gridding.1 = f32[2,256,128]{2,1,0:T(8,128)} custom-call(bf16[2,16384]{1,0:T(2,128)(2,1)} %bitcast.9, s32[1,16384]{1,0:T(1,128)} %bitcast.10, s32[2,16384]{1,0:T(2,128)} %bitcast.7, s32[2,16384]{1,0:T(2,128)} %bitcast.8, bf16[8,128]{1,0:T(8,128)(2,1)} %bitcast.11, f32[1,256]{1,0:T(1,128)} %bitcast.12, f32[1,128]{1,0:T(1,128)} %bitcast.13, ...), custom_call_target="tpu_custom_call" | custom-call | tf_op jit(solution)/shard_map/gridding/pallas_call | solution.py:368
  59.2 1.7 %copy.13 = f32[2,256,128]{2,1,0:T(8,128)} copy(f32[2,256,128]{2,1,0:T(8,128)} %gridding.1) | data formatting | bytes 524288
